TPU v7x, 256 devices: a whole 4x4x8 slice. The times are simulated.
256 devices in a mesh: grp: 8 (over z_hi, core), fsdp: 32 (over y, x, z_lo).
Axes of the slice: x: 4, y: 4, z: 8 (z_hi: 4, z_lo: 2; z = z_hi * 2 + z_lo), core: 2. Of those that a mesh axis runs over, the one named last changes fastest.
Arguments:
- queries: bfloat16 [32, 1024, 4096], P('fsdp', 'grp')
- out_grad: bfloat16 [32, 1024, 4096], P('fsdp', 'grp'), may hold values from -6 to 6
- resp_in: bfloat16 [32, 1024, 5120], P('fsdp', 'grp'), may hold values from -6 to 6
- prompt_in: bfloat16 [32, 512, 5120], P('fsdp', 'grp'), may hold values from -6 to 6
- key_matrix: bfloat16 [5120, 512], P('fsdp'), may hold values from -0.078125 to 0.078125
- value_matrix: bfloat16 [5120, 512], P('fsdp'), may hold values from -0.078125 to 0.078125
- key_gain: float32 [128], replicated, may hold values from 0.1 to 1.9
- seg_prompt: int32 [32, 16], P('fsdp', 'grp'), may hold values from 0 to 7, as said below
- seg_start: int32 [32, 16], P('fsdp', 'grp'), may hold values from 0 to 112, as said below
- seg_len: int32 [32, 16], P('fsdp', 'grp'), may hold values from 1 to 112, as said below
- owner: int32 [32, 8], P('fsdp'), may hold values from 0 to 7, as said below
Outputs:
- query_grad: bfloat16 [32, 1024, 4096], P('fsdp', 'grp')
- resp_grad: bfloat16 [32, 1024, 5120], P('fsdp', 'grp')
- prompt_grad: bfloat16 [32, 512, 5120], P('fsdp', 'grp')
- key_weight_grad: bfloat16 [5120, 512], P('fsdp')
- value_weight_grad: bfloat16 [5120, 512], P('fsdp')
Inputs may be any that keep to these rules, and one draw needn't show every extreme that they name: `owner`: each row of the grp devices of one group is a permutation of 0 to 7. `seg_prompt`: within one group every prompt is named exactly 2 times. `seg_start`: on each device the starts rise, the first is 0, all are multiples of 16, and each response ends no later than the next one starts (the last one within the device's slots). `seg_len`: each response ends within the 16 slots before the next start (or the device's end).
All inputs are finite; a program needn't handle non-finite values.
Results may differ from a plain program's by a relative error of at most 0.04.
The roundings to bfloat16 on the way count: a program that leaves them out, or rounds other values in their place, can miss the bound.
Values may be sent and summed in bfloat16 or wider, within the bound.
A program may use at most 128 MiB of HBM per device.

v0:
```python
import math

import jax
import jax.numpy as jnp
from jax import lax
from jax.sharding import PartitionSpec as P

QUERY_HEADS = 32
KEY_VALUE_HEADS = 4
HEAD_SIZE = 128


rope_base = 1000000.0


def layout(starts, lengths, count_of_rows):
    index_row = jnp.arange(count_of_rows, dtype=jnp.int32)
    segment = jnp.sum((index_row[:, None] >= starts[None, :]).astype(jnp.int32), 1) - 1
    onehot = segment[:, None] == jnp.arange(starts.shape[0], dtype=jnp.int32)[None, :]
    seg_begin = jnp.sum(jnp.where(onehot, starts[None, :], 0), 1)
    seg_size = jnp.sum(jnp.where(onehot, lengths[None, :], 0), 1)
    offset = index_row - seg_begin
    return (segment, offset, offset < seg_size)


def norm_rope(raw, gain, positions):
    how_many = raw.shape[0]
    heads = raw.reshape(how_many, -1, HEAD_SIZE)
    square_mean = jnp.mean(heads * heads, axis=-1, keepdims=True)
    normed = heads * lax.rsqrt(square_mean + 1e-06) * gain
    half_dim = HEAD_SIZE // 2
    frequency = rope_base ** (-jnp.arange(half_dim, dtype=jnp.float32) / half_dim)
    angles = positions.astype(jnp.float32)[:, None] * frequency[None, :]
    cosine = jnp.cos(angles)[:, None, :]
    sines = jnp.sin(angles)[:, None, :]
    lower_half = normed[..., :half_dim]
    upper_half = normed[..., half_dim:]
    turned = jnp.concatenate(
        [lower_half * cosine - upper_half * sines, upper_half * cosine + lower_half * sines], -1
    )
    return turned.reshape(how_many, -1)


def attend(queries, key_tensor, value_tensor, allowed):
    count_of_rows = queries.shape[0]
    heads_per_group = QUERY_HEADS // KEY_VALUE_HEADS
    query_head_count = queries.reshape(count_of_rows, KEY_VALUE_HEADS, heads_per_group, HEAD_SIZE)
    key_head_count = key_tensor.reshape(-1, KEY_VALUE_HEADS, HEAD_SIZE)
    value_head_count = value_tensor.reshape(-1, KEY_VALUE_HEADS, HEAD_SIZE)
    scores = jnp.einsum(
        "rkgd,mkd->kgrm", query_head_count, key_head_count, preferred_element_type=jnp.float32
    ) / math.sqrt(HEAD_SIZE)
    scores = jnp.where(allowed[None, None], scores, -1e30)
    row_max = lax.stop_gradient(jnp.max(scores, axis=-1, keepdims=True))
    weights = jnp.exp(scores - row_max)
    probabilities = (weights / jnp.sum(weights, axis=-1, keepdims=True)).astype(jnp.bfloat16)
    attended = jnp.einsum(
        "kgrm,mkd->rkgd", probabilities, value_head_count, preferred_element_type=jnp.float32
    )
    return attended.reshape(count_of_rows, QUERY_HEADS * HEAD_SIZE)


def back_project(grads, weight):
    return lax.dot_general(
        grads, weight, (((1,), (1,)), ((), ())), preferred_element_type=jnp.float32
    )


def local(
    queries,
    out_grad,
    resp_in,
    prompt_in,
    key_matrix,
    value_matrix,
    key_gain,
    seg_prompt,
    seg_start,
    seg_len,
    owner,
):
    my_queries = queries[0]
    my_cotangent = out_grad[0]
    resp_rows = resp_in[0]
    prompt_rows = prompt_in[0]
    starts = seg_start[0]
    lengths = seg_len[0]
    prompt_ids = seg_prompt[0]
    owners = owner[0]
    count_of_rows = resp_rows.shape[0]
    prompt_len = prompt_rows.shape[0]
    groups = lax.axis_size("grp")
    segments = starts.shape[0]
    key_value_width = key_matrix.shape[1]
    whole_key = lax.all_gather(key_matrix, "fsdp", axis=0, tiled=True)
    whole_value = lax.all_gather(value_matrix, "fsdp", axis=0, tiled=True)
    all_rows = jnp.concatenate([resp_rows, prompt_rows], 0)
    raw_keys = jnp.dot(all_rows, whole_key, preferred_element_type=jnp.float32)
    all_values = jnp.dot(all_rows, whole_value, preferred_element_type=jnp.float32).astype(
        jnp.bfloat16
    )
    segment, offset, usable = layout(starts, lengths, count_of_rows)
    positions = jnp.concatenate([prompt_len + offset, jnp.arange(prompt_len, dtype=jnp.int32)], 0)
    keys_all = norm_rope(raw_keys, key_gain, positions).astype(jnp.bfloat16)
    own_keys = keys_all[:count_of_rows]
    owned_keys = keys_all[count_of_rows:]
    own_values = all_values[:count_of_rows]
    owned_values = all_values[count_of_rows:]
    group_keys, group_values = (
        lax.all_gather(owned_keys, "grp", axis=0, tiled=True),
        lax.all_gather(owned_values, "grp", axis=0, tiled=True),
    )
    slot_list = []
    for which in range(segments):
        picked = jnp.sum(
            jnp.where(jnp.arange(groups, dtype=jnp.int32) == prompt_ids[which], owners, 0)
        )
        slot_list.append(picked * prompt_len)
    seg_keys = jnp.concatenate(
        [lax.dynamic_slice_in_dim(group_keys, place, prompt_len, 0) for place in slot_list], 0
    )
    seg_values = jnp.concatenate(
        [lax.dynamic_slice_in_dim(group_values, place, prompt_len, 0) for place in slot_list], 0
    )
    key_tensor = jnp.concatenate([seg_keys, own_keys], 0)
    value_tensor = jnp.concatenate([seg_values, own_values], 0)
    index_row = jnp.arange(count_of_rows, dtype=jnp.int32)
    resp_ok = (
        (segment[:, None] == segment[None, :])
        & (index_row[None, :] <= index_row[:, None])
        & usable[None, :]
    )
    block_of_key = jnp.arange(segments * prompt_len, dtype=jnp.int32) // prompt_len
    prompt_ok = segment[:, None] == block_of_key[None, :]
    allowed = jnp.concatenate([prompt_ok, resp_ok], 1)
    _, backward = jax.vjp(
        lambda qarg, karg, varg: attend(qarg, karg, varg, allowed),
        my_queries,
        key_tensor,
        value_tensor,
    )
    cotangent = my_cotangent.astype(jnp.float32) * usable[:, None].astype(jnp.float32)
    query_grad, key_grad, value_grad = backward(cotangent)
    split_at = segments * prompt_len
    part_keys = jnp.zeros((groups * prompt_len, key_value_width), jnp.float32)
    part_values = jnp.zeros((groups * prompt_len, key_value_width), jnp.float32)
    for which in range(segments):
        place = slot_list[which]
        lower = which * prompt_len
        upper = lower + prompt_len
        current = lax.dynamic_slice_in_dim(part_keys, place, prompt_len, 0)
        part_keys = lax.dynamic_update_slice_in_dim(
            part_keys, current + key_grad[lower:upper].astype(jnp.float32), place, 0
        )
        current = lax.dynamic_slice_in_dim(part_values, place, prompt_len, 0)
        part_values = lax.dynamic_update_slice_in_dim(
            part_values, current + value_grad[lower:upper].astype(jnp.float32), place, 0
        )
    prompt_kgrad, prompt_vgrad = (
        lax.psum_scatter(
            part_keys.astype(jnp.bfloat16), "grp", scatter_dimension=0, tiled=True
        ).astype(jnp.float32),
        lax.psum_scatter(
            part_values.astype(jnp.bfloat16), "grp", scatter_dimension=0, tiled=True
        ).astype(jnp.float32),
    )
    _, key_back = jax.vjp(lambda raw: norm_rope(raw, key_gain, positions), raw_keys)
    key_cot = jnp.concatenate([key_grad[split_at:].astype(jnp.float32), prompt_kgrad], 0)
    raw_kgrad = key_back(key_cot)[0].astype(jnp.bfloat16)
    value_all = jnp.concatenate([value_grad[split_at:], prompt_vgrad.astype(jnp.bfloat16)], 0)
    input_grad = (back_project(raw_kgrad, whole_key) + back_project(value_all, whole_value)).astype(
        jnp.bfloat16
    )
    stacked = jnp.concatenate([raw_kgrad, value_all], 1)
    summed = lax.psum_scatter(
        lax.dot_general(
            all_rows, stacked, (((0,), (0,)), ((), ())), preferred_element_type=jnp.float32
        ).astype(jnp.bfloat16),
        "fsdp",
        scatter_dimension=0,
        tiled=True,
    ).astype(jnp.float32)
    key_total, value_total = (
        lax.psum(summed[:, :key_value_width].astype(jnp.bfloat16), "grp").astype(jnp.float32),
        lax.psum(summed[:, key_value_width:].astype(jnp.bfloat16), "grp").astype(jnp.float32),
    )
    key_out = key_total.astype(jnp.bfloat16)
    value_out = value_total.astype(jnp.bfloat16)
    return (
        query_grad[None],
        input_grad[:count_of_rows][None],
        input_grad[count_of_rows:][None],
        key_out,
        value_out,
    )


def solution(mesh):
    in_specs = (
        P("fsdp", "grp", None),
        P("fsdp", "grp", None),
        P("fsdp", "grp", None),
        P("fsdp", "grp", None),
        P("fsdp", None),
        P("fsdp", None),
        P(),
        P("fsdp", "grp"),
        P("fsdp", "grp"),
        P("fsdp", "grp"),
        P("fsdp", None),
    )
    out_specs = (
        P("fsdp", "grp", None),
        P("fsdp", "grp", None),
        P("fsdp", "grp", None),
        P("fsdp", None),
        P("fsdp", None),
    )
    return jax.shard_map(local, mesh=mesh, in_specs=in_specs, out_specs=out_specs, check_vma=False)
```

profile of v0, /device:TPU:1, one launch (start us, length us, event | category | flops | bytes accessed | tf_op | source)
XLA Modules:
  0.0 818.3 jit_solution(16423369886203099714)
XLA Ops:
  8.7 1.3 fusion.69
  10.0 2.6 fusion.52
  13.9 1.4 copy.171
  15.4 1.5 copy.155
  19.7 145.1 %all-gather.5.cloned.1.call-done = bf16[5120,512]{1,0:T(8,128)(2,1)} async-done(((bf16[160,512]{1,0:T(8,128)(2,1)}), bf16[5120,512]{1,0:T(8,128)(2,1)}) %all-gather.5.cloned.1.call-update) | async-done | bytes 5242896 | tf_op jit(solution)/shard_map/all_gather | solution.py:95
  164.8 5.0 fusion.36
  177.7 159.0 %all-gather.3.cloned.1.call-done = bf16[5120,512]{1,0:T(8,128)(2,1)} async-done(((bf16[160,512]{1,0:T(8,128)(2,1)}), bf16[5120,512]{1,0:T(8,128)(2,1)}) %all-gather.3.cloned.1.call-update) | async-done | bytes 5242896 | tf_op jit(solution)/shard_map/all_gather | solution.py:96
  336.8 4.3 convolution_convert_fusion.2
  341.7 1.7 copy.126
  344.2 38.1 %all_gather.15 = bf16[512,512]{1,0:T(8,128)(2,1)S(1)} all-gather(bf16[64,512]{1,0:T(8,128)(2,1)S(1)} %bitcast.163), channel_id=1, replica_groups=mesh['grp'=8,'fsdp'=32] {'grp'}, dimensions={0}, use_global_device_ids=true | all-gather | bytes 589824 | tf_op jit(solution)/shard_map/all_gather | solution.py:110
  383.0 1.6 copy.165
  384.6 1.6 copy.164
  387.4 2.1 fusion.8
  389.6 1.9 copy-done
  391.5 1.7 fusion.9
  393.8 14.9 %all_gather.13 = bf16[512,512]{1,0:T(8,128)(2,1)S(1)} all-gather(bf16[64,512]{1,0:T(8,128)(2,1)S(1)} %slice-done.2), channel_id=1, replica_groups=mesh['grp'=8,'fsdp'=32] {'grp'}, dimensions={0}, use_global_device_ids=true | all-gather | bytes 589824 | tf_op jit(solution)/shard_map/all_gather | solution.py:111
  409.5 1.7 reshape.200
  411.2 4.2 fusion.7
  415.5 2.1 fusion.5
  420.5 3.8 fusion.28
  430.5 21.6 %reduce-scatter.10.cloned.1.call-done = bf16[64,512]{1,0:T(8,128)(2,1)} async-done(((bf16[512,512]{1,0:T(8,128)(2,1)}), bf16[64,512]{1,0:T(8,128)(2,1)}) %reduce-scatter.10.cloned.1.call-update) | async-done | bytes 65552
  455.8 1.4 multiply_add_fusion.1
  458.6 1.6 fusion.42
  460.4 30.3 %reduce-scatter.12.cloned.1.call-done = bf16[64,512]{1,0:T(8,128)(2,1)} async-done(((bf16[512,512]{1,0:T(8,128)(2,1)}), bf16[64,512]{1,0:T(8,128)(2,1)}) %reduce-scatter.12.cloned.1.call-update) | async-done | bytes 65552
  491.7 8.6 %convolution_convert_fusion = bf16[5120,1024]{1,0:T(8,128)(2,1)} fusion(bf16[64,5120]{1,0:T(8,128)(2,1)} %bitcast.159, bf16[128,5120]{1,0:T(8,128)(2,1)} %bitcast.152, bf16[64,512]{0,1:T(8,128)(2,1)S(1)} %copy.163, bf16[128,512]{0,1:T(8,128)(2,1)} %bitcast.153, bf16[192,512]{0,1:T(8,128)(2,1)S(1)} %copy.144), kind=kOutput, calls=%fused_computation | convolution fusion | flops 2023620608 | bytes 12845056 | tf_op jit(solution)/shard_map/dot_general | solution.py:176
  503.4 4.5 fusion.62
  507.9 4.5 fusion
  513.5 222.0 %reduce-scatter.8.cloned.1.call-done = bf16[160,1024]{1,0:T(8,128)(2,1)} async-done(((bf16[5120,1024]{1,0:T(8,128)(2,1)}), bf16[160,1024]{1,0:T(8,128)(2,1)}) %reduce-scatter.8.cloned.1.call-update) | async-done | bytes 327696 | tf_op jit(solution)/shard_map/reduce_scatter | solution.py:175
  735.6 1.7 fusion.66
  738.2 70.1 %all-reduce.5.cloned.1.call-done = (bf16[160,512]{1,0:T(8,128)(2,1)}, bf16[160,512]{1,0:T(8,128)(2,1)}) async-done(((bf16[160,512]{1,0:T(8,128)(2,1)}, bf16[160,512]{1,0:T(8,128)(2,1)}), (bf16[160,512]{1,0:T(8,128)(2,1)}, bf16[160,512]{1,0:T(8,128)(2,1)})) %all-reduce.5.cloned.1.call-update) | async-done | bytes 327696 | tf_op jit(solution)/shard_map/psum | solution.py:184
  808.3 1.6 copy.196
  809.9 1.6 copy.197
  (119 shorter events, 37.2 us)
Async XLA Ops:
  7.2 9.7 %copy-start.19 = (s32[1,2]{1,0:T(1,128)S(1)}, s32[1,2]{1,0:T(1,128)}, u32[]{:S(2)}) copy-start(s32[1,2]{1,0:T(1,128)} %param.19) | copy-start | bytes 28
  7.2 9.8 %copy-start.20 = (s32[1,2]{1,0:T(1,128)S(1)}, s32[1,2]{1,0:T(1,128)}, u32[]{:S(2)}) copy-start(s32[1,2]{1,0:T(1,128)} %param.20) | copy-start | bytes 28
  7.2 157.7 %all-gather.5.cloned.1.call-start = ((), (), s32[]{:S(2)}) async-start(), calls=%async_computation.4 | async-start | bytes 5406720 | tf_op jit(solution)/shard_map/all_gather | solution.py:95
  7.9 328.8 %all-gather.3.cloned.1.call-start = ((), (), s32[]{:S(2)}) async-start(), calls=%async_computation.3 | async-start | bytes 5406720 | tf_op jit(solution)/shard_map/all_gather | solution.py:96
  8.7 443.3 %reduce-scatter.10.cloned.1.call-start = ((), (), s32[]{:S(2)}) async-start(), calls=%async_computation.6 | async-start | bytes 589824
  16.9 394.4 %copy-start.5 = (f32[1,128,4096]{1,2,0:T(8,128)}, f32[1,128,4096]{1,2,0:T(8,128)S(1)}, u32[]{:S(2)}) copy-start(f32[1,128,4096]{1,2,0:T(8,128)S(1)} %copy.155) | copy-start | bytes 6291460
  164.8 8.8 %copy-start.17 = (f32[128]{0:T(128)S(1)}, f32[128]{0:T(128)}, u32[]{:S(2)}) copy-start(f32[128]{0:T(128)} %param.17) | copy-start | bytes 1540
  172.9 168.1 %copy-start.15 = (f32[192,4]{0,1:T(4,128)}, f32[192,4]{0,1:T(4,128)S(1)}, u32[]{:S(2)}) copy-start(f32[192,4]{0,1:T(4,128)S(1)} %copy.122) | copy-start | bytes 9220
  341.0 0.7 copy-start.10
  386.2 5.3 copy-start.11
  387.4 5.8 copy-start.2
  387.4 6.4 slice-start.2
  387.4 21.4 %slice-start.1 = ((bf16[192,512]{1,0:T(8,128)(2,1)}), bf16[128,512]{1,0:T(8,128)(2,1)S(1)}, s32[]{:S(2)}) async-start(bf16[192,512]{1,0:T(8,128)(2,1)} %copy-done.10), calls=%async_computation.10 | async-start | bytes 262144 | tf_op jit(solution)/shard_map/slice | solution.py:107
  389.6 1.9 copy-start
  393.2 15.6 %copy-start.12 = (f32[4,8,128]{2,1,0:T(8,128)}, f32[4,8,128]{2,1,0:T(8,128)S(1)}, u32[]{:S(2)}) copy-start(f32[4,8,128]{2,1,0:T(8,128)S(1)} %fusion.9) | copy-start | bytes 49156
  411.2 4.3 copy-start.1
  411.2 4.3 copy-start.13
  411.2 4.3 copy-start.14
  418.7 0.7 copy-start.9
  420.3 4.1 slice-start
  420.3 70.4 %reduce-scatter.12.cloned.1.call-start = ((), (), s32[]{:S(2)}) async-start(), calls=%async_computation.7 | async-start | bytes 589824
  427.5 29.7 %copy-start.18 = (f32[128]{0:T(128)S(1)}, f32[128]{0:T(128)}, u32[]{:S(2)}) copy-start(f32[128]{0:T(128)} %param.17) | copy-start | bytes 1540
  429.5 28.3 %copy-start.16 = (f32[192,4]{0,1:T(4,128)S(1)}, f32[192,4]{0,1:T(4,128)}, u32[]{:S(2)}) copy-start(f32[192,4]{0,1:T(4,128)} %copy-done.15) | copy-start | bytes 9220
  430.4 305.2 %reduce-scatter.8.cloned.1.call-start = ((), (), s32[]{:S(2)}) async-start(), calls=%async_computation.5 | async-start | bytes 10813440 | tf_op jit(solution)/shard_map/reduce_scatter | solution.py:175
  460.3 40.1 %copy-start.4 = (bf16[192,4,128]{2,1,0:T(4,128)(2,1)}, bf16[192,4,128]{2,1,0:T(4,128)(2,1)S(1)}, u32[]{:S(2)}) copy-start(bf16[192,4,128]{2,1,0:T(4,128)(2,1)S(1)} %fusion.42) | copy-start | bytes 589828
  491.7 8.6 %copy-start.7 = (bf16[64,512]{0,1:T(8,128)(2,1)}, bf16[64,512]{0,1:T(8,128)(2,1)S(1)}, u32[]{:S(2)}) copy-start(bf16[64,512]{0,1:T(8,128)(2,1)S(1)} %copy.163) | copy-start | bytes 196612
  500.3 1.0 copy-start.3
  500.3 308.0 %all-reduce.5.cloned.1.call-start = ((), (), s32[]{:S(2)}) async-start(), calls=%async_computation.8 | async-start | bytes 655360 | tf_op jit(solution)/shard_map/psum | solution.py:184
  503.4 4.5 copy-start.6
  503.4 4.5 copy-start.8
Sparse Core Ops, SparseCore 0:
  9.8 154.9 all-gather.4
  166.6 170.0 all-gather.2
  420.4 31.5 reduce-scatter.9
  455.1 35.5 reduce-scatter.11
  500.4 235.0 reduce-scatter.7
  738.6 69.6 all-reduce.4
where the time goes:
time: 820 us; the launch traced here: 818 us
  waiting for transfers between devices  650 us (79%)
  blocking collectives  53 us (6%)
  matrix products  38.9 us (5%)
  local copies, waits for them, and re-layouts  36.6 us (4%)
  other arithmetic  23.9 us (3%)
  between operations  16 us (2%)
    reduce_scatter x1, waiting for transfers between devices, local(): lax.psum_scatter(lax.dot_general(all_rows, stacked, (((0,), (0,)), ((), (...  222 us
    all_gather x1, waiting for transfers between devices, local(): whole_value = lax.all_gather(value_matrix, 'fsdp', axis=0, tiled=True)  159 us
    all_gather x1, waiting for transfers between devices, local(): whole_key = lax.all_gather(key_matrix, 'fsdp', axis=0, tiled=True)  145 us
    psum x1, waiting for transfers between devices, local(): lax.psum(summed[:, :key_value_width].astype(jnp.bfloat16), 'grp')  70.1 us
    unnamed x8, waiting for transfers between devices  53.3 us
    all_gather x1, blocking collectives, local(): lax.all_gather(owned_keys, 'grp', axis=0, tiled=True)  38.1 us
    unnamed x54, local copies, waits for them, and re-layouts  17.8 us
  transfers between devices with their start and end apart: 6, of which 6 were waited for; matrix products, arithmetic and copies ran while one was open for 7% of the time, Pallas kernels for 0%

commit v1 on v0

v1 whole, which is shorter than its diff:
```python
import functools
import math

import jax
import jax.numpy as jnp
import numpy as np
from jax import lax
from jax.experimental import pallas as pl
from jax.experimental.pallas import tpu as pltpu
from jax.sharding import PartitionSpec as P

MESH = pl.DeviceIdType.MESH
ANY = pl.BlockSpec(memory_space=pl.ANY)
SMEM = pl.BlockSpec(memory_space=pltpu.SMEM)
VMEM = pl.BlockSpec(memory_space=pltpu.VMEM)
VMEM_LIMIT = 52 * 1024 * 1024

WIDTH = 5120
HEAD = 128
ROWS = 160
HALF = 80
TOK = 128
PRO = 64
DEV = TOK + PRO
SCALE = 1.0 / math.sqrt(HEAD)
BASE = 1000000.0
bf16 = jnp.bfloat16
f32 = jnp.float32


def rotary_tables():
    frequency = np.float32(BASE) ** (-np.arange(64, dtype=np.float32) / np.float32(64))
    angles = np.arange(-128, 192, dtype=np.float32)[:, None] * frequency[None, :].astype(np.float32)
    angles = angles.astype(np.float32).astype(np.float64)
    cos, sin = np.cos(angles), np.sin(angles)
    return (
        np.concatenate([cos, cos], 1).astype(np.float32),
        np.concatenate([-sin, sin], 1).astype(np.float32),
    )


class Place:
    def __init__(self):
        g, f = lax.axis_index("grp"), lax.axis_index("fsdp")
        self.core, self.zh = lax.rem(g, 2), lax.div(g, 2)
        self.zl = lax.rem(f, 2)
        self.x = lax.rem(lax.div(f, 2), 4)
        self.y = lax.div(f, 8)
        self.z = self.zh * 2 + self.zl

    def at(self, y=None, x=None, z=None, core=None):
        y = self.y if y is None else y
        x = self.x if x is None else x
        z = self.z if z is None else z
        core = self.core if core is None else core
        return {"grp": lax.div(z, 2) * 2 + core, "fsdp": (y * 4 + x) * 2 + lax.rem(z, 2)}

    def ring_x(self):
        return self.x, self.at(x=lax.rem(self.x + 3, 4)), self.at(x=lax.rem(self.x + 1, 4))

    def ring_y(self):
        return self.y, self.at(y=lax.rem(self.y + 3, 4)), self.at(y=lax.rem(self.y + 1, 4))

    def ring_zh(self):
        return self.zh, self.at(z=lax.rem(self.z + 6, 8)), self.at(z=lax.rem(self.z + 2, 8))

    def near_z(self):
        return self.at(z=lax.rem(self.z + 7, 8)), self.at(z=lax.rem(self.z + 1, 8))

    def partner(self):
        return self.at(core=1 - self.core)


def greet(devices):
    barrier = pltpu.get_barrier_semaphore()
    for device in devices:
        pl.semaphore_signal(barrier, inc=1, device_id=device, device_id_type=MESH)
    pl.semaphore_wait(barrier, len(devices))


class Links:
    def __init__(self, send, recv):
        self.send, self.recv, self.used, self.sent = send, recv, 0, []

    def take(self):
        self.used += 1
        return self.used - 1

    def copy(self, number, src, dst, device):
        return pltpu.make_async_remote_copy(
            src_ref=src,
            dst_ref=dst,
            send_sem=self.send.at[number],
            recv_sem=self.recv.at[number],
            device_id=device,
            device_id_type=MESH,
        )

    def start(self, number, src, dst, device):
        made = self.copy(number, src, dst, device)
        made.start()
        self.sent.append(made)

    def arrived(self, number, dst, device):
        self.copy(number, dst, dst, device).wait_recv()

    def drain(self):
        for made in self.sent:
            made.wait_send()
        self.sent = []


class Gather4:
    def __init__(self, links, ring, view, half, own=None):
        self.links, self.view, self.half = links, view, half
        self.me, self.minus, self.plus = ring
        self.own = view(self.me) if own is None else own
        self.n = [links.take() for _ in range(4)]

    def begin(self):
        self.links.start(self.n[0], self.own, self.view(self.me), self.plus)
        self.links.start(self.n[1], self.own, self.view(self.me), self.minus)

    def forward(self):
        left, right = lax.rem(self.me + 3, 4), lax.rem(self.me + 1, 4)
        self.links.arrived(self.n[0], self.view(left), self.plus)
        self.links.start(self.n[2], self.half(left, 0), self.half(left, 0), self.plus)
        self.links.arrived(self.n[1], self.view(right), self.minus)
        self.links.start(self.n[3], self.half(right, 1), self.half(right, 1), self.minus)

    def finish(self):
        across = lax.rem(self.me + 2, 4)
        self.links.arrived(self.n[2], self.half(across, 0), self.plus)
        self.links.arrived(self.n[3], self.half(across, 1), self.minus)


class Reduce4:
    def __init__(self, links, ring, part, slot, add):
        self.links, self.part, self.slot, self.add = links, part, slot, add
        self.me, self.minus, self.plus = ring
        self.n = [links.take() for _ in range(6)]

    def begin(self):
        across = lax.rem(self.me + 2, 4)
        left, right = lax.rem(self.me + 3, 4), lax.rem(self.me + 1, 4)
        part, slot, n = self.part, self.slot, self.n
        self.links.start(n[0], part(across, 0), slot(0), self.plus)
        self.links.start(n[1], part(across, 1), slot(1), self.minus)
        self.links.start(n[2], part(right, 1), slot(2), self.plus)
        self.links.start(n[3], part(left, 0), slot(3), self.minus)

    def mid(self):
        left, right = lax.rem(self.me + 3, 4), lax.rem(self.me + 1, 4)
        part, slot, n = self.part, self.slot, self.n
        self.links.arrived(n[0], slot(0), self.plus)
        self.add(slot(0), [slot(0), part(right, 0)])
        self.links.start(n[4], slot(0), slot(4), self.plus)
        self.links.arrived(n[1], slot(1), self.minus)
        self.add(slot(1), [slot(1), part(left, 1)])
        self.links.start(n[5], slot(1), slot(5), self.minus)

    def finish(self, out):
        part, slot, n = self.part, self.slot, self.n
        self.links.arrived(n[3], slot(3), self.minus)
        self.links.arrived(n[4], slot(4), self.plus)
        self.add(out(0), [part(self.me, 0), slot(3), slot(4)])
        self.links.arrived(n[2], slot(2), self.plus)
        self.links.arrived(n[5], slot(5), self.minus)
        self.add(out(1), [part(self.me, 1), slot(2), slot(5)])


def add_block(dst, terms):
    total = terms[0][...].astype(f32)
    for term in terms[1:]:
        total = total + term[...].astype(f32)
    dst[...] = total.astype(dst.dtype)


def add_blocks(dst, terms):
    def body(i, carry):
        total = terms[0][i].astype(f32)
        for term in terms[1:]:
            total = total + term[i].astype(f32)
        dst[i] = total.astype(dst.dtype)
        return carry

    lax.fori_loop(0, dst.shape[0], body, 0)


def remote_params(number):
    return pltpu.CompilerParams(
        collective_id=number, has_side_effects=True, vmem_limit_bytes=VMEM_LIMIT
    )


LOCAL = pltpu.CompilerParams(vmem_limit_bytes=VMEM_LIMIT)


GATHER_COPIES = 64


def gather_kernel(kw, vw, resp, prompt, q, og, info, W, X, Q, OG, INFO, send, recv, local):
    me = Place()
    core, partner = me.core, me.partner()
    near_minus, near_plus = me.near_z()
    _, xm, xp = me.ring_x()
    _, ym, yp = me.ring_y()
    greet([xm, xp, ym, yp, near_minus, near_plus, partner])
    links = Links(send, recv)

    def columns(matrix, j):
        return matrix.at[:, pl.ds(pl.multiple_of((core * 2 + j) * HEAD, HEAD), HEAD)]

    own = [columns(kw, 0), columns(kw, 1), columns(vw, 0), columns(vw, 1)]
    x, y, zl = me.x, me.y, me.zl
    rows = lambda h: pl.ds(h * HALF, HALF)

    ax = Gather4(links, me.ring_x(), lambda c: W.at[0, y, c, zl], lambda c, h: W.at[0, y, c, zl, rows(h)], own[0])
    ay = Gather4(links, me.ring_y(), lambda c: W.at[0, c, :, zl], lambda c, h: W.at[0, c, :, zl, rows(h)])
    by = Gather4(links, me.ring_y(), lambda c: W.at[1, c, x, zl], lambda c, h: W.at[1, c, x, zl, rows(h)], own[1])
    bx = Gather4(links, me.ring_x(), lambda c: W.at[1, :, c, zl], lambda c, h: W.at[1, :, c, zl, rows(h)])
    cx = Gather4(links, me.ring_x(), lambda c: W.at[2, y, c], lambda c, h: W.at[2, y, c, h])
    cy = Gather4(links, me.ring_y(), lambda c: W.at[2, c], lambda c, h: W.at[2, c, :, h])
    dy = Gather4(links, me.ring_y(), lambda c: W.at[3, c, x], lambda c, h: W.at[3, c, x, h])
    dx = Gather4(links, me.ring_x(), lambda c: W.at[3, :, c], lambda c, h: W.at[3, :, c, h])
    zn = [(links.take(), links.take()) for _ in range(4)]

    def z_begin(t, src):
        links.start(zn[t][0], src(0), z_view(t, zl, 0), near_plus)
        links.start(zn[t][1], src(1), z_view(t, zl, 1), near_minus)

    def z_finish(t):
        links.arrived(zn[t][0], z_view(t, 1 - zl, 0), near_plus)
        links.arrived(zn[t][1], z_view(t, 1 - zl, 1), near_minus)

    def z_view(t, which, h):
        if t < 2:
            return W.at[t, :, :, which, rows(h)]
        return W.at[t, y, x, which, rows(h)]

    ax.begin()
    by.begin()
    for t in (2, 3):
        matrix_half = lambda h, t=t: vw.at[rows(h), pl.ds(pl.multiple_of((core * 2 + t - 2) * HEAD, HEAD), HEAD)]
        z_begin(t, matrix_half)

    locals_ = []

    def here(src, dst):
        made = pltpu.make_async_copy(src, dst, local.at[len(locals_)])
        made.start()
        locals_.append(made)

    for t in range(4):
        here(own[t], W.at[t, y, x, zl])
    swaps = []

    def swap(src, dst_mine, dst_theirs):
        number = links.take()
        links.start(number, src, dst_mine, partner)
        swaps.append((number, dst_theirs))

    mine = pl.ds(pl.multiple_of(core * 2048, 2048), 2048)
    theirs = pl.ds(pl.multiple_of((1 - core) * 2048, 2048), 2048)
    swap(info, INFO.at[core], INFO.at[1 - core])
    swap(resp.at[0], X.at[core, pl.ds(0, TOK)], X.at[1 - core, pl.ds(0, TOK)])
    swap(prompt.at[0], X.at[core, pl.ds(TOK, PRO)], X.at[1 - core, pl.ds(TOK, PRO)])
    swap(q.at[0, :, theirs], Q.at[core], Q.at[1 - core])
    swap(og.at[0, :, theirs], OG.at[core], OG.at[1 - core])
    here(info, INFO.at[core])
    here(resp.at[0], X.at[core, pl.ds(0, TOK)])
    here(prompt.at[0], X.at[core, pl.ds(TOK, PRO)])
    here(q.at[0, :, mine], Q.at[core])
    here(og.at[0, :, mine], OG.at[core])

    ax.forward()
    by.forward()
    for made in locals_[:4]:
        made.wait()
    z_finish(2)
    cx.begin()
    z_finish(3)
    dy.begin()
    ax.finish()
    ay.begin()
    by.finish()
    bx.begin()
    cx.forward()
    dy.forward()
    cx.finish()
    cy.begin()
    dy.finish()
    dx.begin()
    ay.forward()
    bx.forward()
    ay.finish()
    z_begin(0, lambda h: z_view(0, zl, h))
    bx.finish()
    z_begin(1, lambda h: z_view(1, zl, h))
    cy.forward()
    dx.forward()
    cy.finish()
    dx.finish()
    z_finish(0)
    z_finish(1)
    for number, landing in swaps:
        links.arrived(number, landing, partner)
    for made in locals_[4:]:
        made.wait()
    links.drain()
    assert links.used <= GATHER_COPIES


def gather(kw, vw, resp, prompt, q, og, info):
    return pl.pallas_call(
        gather_kernel,
        out_shape=(
            jax.ShapeDtypeStruct((4, 4, 4, 2, ROWS, HEAD), bf16),
            jax.ShapeDtypeStruct((2, DEV, WIDTH), bf16),
            jax.ShapeDtypeStruct((2, TOK, 2048), bf16),
            jax.ShapeDtypeStruct((2, TOK, 2048), bf16),
            jax.ShapeDtypeStruct((2, 8, 128), jnp.int32),
        ),
        in_specs=[ANY] * 7,
        out_specs=(ANY,) * 5,
        scratch_shapes=[
            pltpu.SemaphoreType.DMA((GATHER_COPIES,)),
            pltpu.SemaphoreType.DMA((GATHER_COPIES,)),
            pltpu.SemaphoreType.DMA((16,)),
        ],
        compiler_params=remote_params(1),
        name="gather",
    )(kw, vw, resp, prompt, q, og, info)


K_STEP = 1024


def swap_halves(a):
    return pltpu.roll(a, 64, 1)


def tables_of(info, d, cos, sin):
    start = info[d, 0, 3]
    late = pl.multiple_of(192 - start, 16)
    row = lax.broadcasted_iota(jnp.int32, (TOK, HEAD), 0)
    out = []
    for table in (cos, sin):
        first = table[pl.ds(192, TOK), :]
        second = table[pl.ds(late, TOK), :]
        out.append(jnp.concatenate([jnp.where(row < start, first, second), table[pl.ds(128, PRO), :]], 0))
    return out


def project_kernel(info, X, W, cos, sin, gain, raw, keys, vals, pkv, acc):
    step = pl.program_id(0)
    left = jnp.concatenate([X[0], X[1]], 0)
    right = jnp.concatenate([W[t] for t in range(4)], 1)
    part = jnp.dot(left, right, preferred_element_type=f32)

    @pl.when(step == 0)
    def _():
        acc[...] = part

    @pl.when(step > 0)
    def _():
        acc[...] += part

    @pl.when(step == pl.num_programs(0) - 1)
    def _():
        for d in range(2):
            c, s = tables_of(info, d, cos, sin)
            for j in range(2):
                k = acc[pl.ds(d * DEV, DEV), pl.ds(j * HEAD, HEAD)]
                raw[j, d] = k
                square = jnp.mean(k * k, axis=1, keepdims=True)
                normed = k * lax.rsqrt(square + 1e-06) * gain[...]
                turned = (normed * c + swap_halves(normed) * s).astype(bf16)
                keys[j, d] = turned
                pkv[j, d] = turned[TOK:]
                v = acc[pl.ds(d * DEV, DEV), pl.ds((2 + j) * HEAD, HEAD)].astype(bf16)
                vals[j, d] = v
                pkv[2 + j, d] = v[TOK:]


def project(info, X, W, cos, sin, gain):
    return pl.pallas_call(
        project_kernel,
        out_shape=(
            jax.ShapeDtypeStruct((2, 2, DEV, HEAD), f32),
            jax.ShapeDtypeStruct((2, 2, DEV, HEAD), bf16),
            jax.ShapeDtypeStruct((2, 2, DEV, HEAD), bf16),
            jax.ShapeDtypeStruct((4, 2, PRO, HEAD), bf16),
        ),
        grid=(WIDTH // K_STEP,),
        in_specs=[
            SMEM,
            pl.BlockSpec((2, DEV, K_STEP), lambda i: (0, 0, i)),
            pl.BlockSpec((4, K_STEP, HEAD), lambda i: (0, i, 0)),
            VMEM,
            VMEM,
            VMEM,
        ],
        out_specs=(VMEM,) * 4,
        scratch_shapes=[pltpu.VMEM((2 * DEV, 512), f32)],
        compiler_params=LOCAL,
        name="project",
    )(info, X, W, cos, sin, gain)


SHARE_COPIES = 8


def share_kernel(pkv, W, everyone, W2, send, recv, local):
    me = Place()
    ring, partner = me.ring_zh(), me.partner()
    greet([ring[1], ring[2], partner])
    links = Links(send, recv)
    own = pltpu.make_async_copy(pkv, everyone.at[me.zh], local)
    own.start()
    going = Gather4(
        links, ring, lambda c: everyone.at[c], lambda c, h: everyone.at[c, pl.ds(2 * h, 2)], pkv
    )
    going.begin()
    weights = links.take()
    links.start(weights, W, W2, partner)
    going.forward()
    going.finish()
    own.wait()
    links.arrived(weights, W2, partner)
    links.drain()


def share(pkv, W):
    return pl.pallas_call(
        share_kernel,
        out_shape=(
            jax.ShapeDtypeStruct((4, 4, 2, PRO, HEAD), bf16),
            jax.ShapeDtypeStruct((4, 4, 4, 2, ROWS, HEAD), bf16),
        ),
        in_specs=[ANY, ANY],
        out_specs=(ANY, ANY),
        scratch_shapes=[
            pltpu.SemaphoreType.DMA((SHARE_COPIES,)),
            pltpu.SemaphoreType.DMA((SHARE_COPIES,)),
            pltpu.SemaphoreType.DMA,
        ],
        compiler_params=remote_params(2),
        name="share",
    )(pkv, W)


def attention_kernel(info, everyone, keys, vals, Q, OG, QG, RG, PP, probs, slopes, queries, cots, parts):
    d, j = pl.program_id(0), pl.program_id(1)

    @pl.when((d == 0) & (j == 0))
    def _():
        parts[...] = jnp.zeros_like(parts)

    slots = [info[d, 0, 0], info[d, 0, 1]]
    start, lens = info[d, 0, 3], [info[d, 0, 4], info[d, 0, 5]]
    places = [(lax.div(s, 2), lax.rem(s, 2)) for s in slots]
    K = jnp.concatenate([everyone[zh, j, c] for zh, c in places] + [keys[0, 0, :TOK]], 0)
    V = jnp.concatenate([everyone[zh, 2 + j, c] for zh, c in places] + [vals[0, 0, :TOK]], 0)

    key = lax.broadcasted_iota(jnp.int32, (2 * TOK, TOK), 0)
    row = lax.broadcasted_iota(jnp.int32, (2 * TOK, TOK), 1)
    late = row >= start
    first = jnp.where(late, start, 0)
    end = jnp.where(late, start + lens[1], lens[0])
    from_key = jnp.where(key < TOK, jnp.where(late, PRO, 0), first + TOK)
    to_key = jnp.where(key < TOK, jnp.where(late, TOK, PRO), jnp.minimum(end, row + 1) + TOK)
    allowed = (key >= from_key) & (key < to_key)
    line = lax.broadcasted_iota(jnp.int32, (TOK, HEAD), 0)
    used = line < jnp.where(line >= start, start + lens[1], lens[0])

    for h in range(8):
        lanes = pl.ds(h * HEAD, HEAD)
        block = pl.ds(h * TOK, TOK)
        q = Q[0, :, lanes]
        cot = jnp.where(used, OG[0, :, lanes].astype(f32), 0.0).astype(bf16)
        queries[block, :] = q
        cots[block, :] = cot
        scores = lax.dot_general(K, q, (((1,), (1,)), ((), ())), preferred_element_type=f32)
        scores = jnp.where(allowed, scores * SCALE, -1e30)
        top = jnp.max(scores, axis=0, keepdims=True)
        weights = jnp.exp(scores - top)
        prob = weights / jnp.sum(weights, axis=0, keepdims=True)
        probs[:, block] = prob.astype(bf16)
        slope = lax.dot_general(V, cot, (((1,), (1,)), ((), ())), preferred_element_type=f32)
        slope = slope.astype(bf16).astype(f32)
        inner = jnp.sum(slope * prob, axis=0, keepdims=True)
        back = (prob * (slope - inner) * SCALE).astype(bf16)
        slopes[:, block] = back
        QG[0, :, lanes] = lax.dot_general(
            back, K, (((0,), (0,)), ((), ())), preferred_element_type=f32
        ).astype(bf16)
    dv = jnp.dot(probs[...], cots[...], preferred_element_type=f32)
    dk = jnp.dot(slopes[...], queries[...], preferred_element_type=f32)
    RG[0, 0, 0] = dk[TOK:].astype(bf16)
    RG[0, 0, 1] = dv[TOK:].astype(bf16)
    for s, (zh, c) in enumerate(places):
        parts[zh, j, c] += dk[s * PRO : (s + 1) * PRO]
        parts[zh, 2 + j, c] += dv[s * PRO : (s + 1) * PRO]

    @pl.when((d == 1) & (j == 1))
    def _():
        PP[...] = parts[...].astype(bf16)


def attention(info, everyone, keys, vals, Q, OG):
    return pl.pallas_call(
        attention_kernel,
        out_shape=(
            jax.ShapeDtypeStruct((2, TOK, 2048), bf16),
            jax.ShapeDtypeStruct((2, 2, 2, TOK, HEAD), bf16),
            jax.ShapeDtypeStruct((4, 4, 2, PRO, HEAD), bf16),
        ),
        grid=(2, 2),
        in_specs=[
            SMEM,
            VMEM,
            pl.BlockSpec((1, 1, DEV, HEAD), lambda d, j: (j, d, 0, 0)),
            pl.BlockSpec((1, 1, DEV, HEAD), lambda d, j: (j, d, 0, 0)),
            pl.BlockSpec((1, TOK, 1024), lambda d, j: (d, 0, j)),
            pl.BlockSpec((1, TOK, 1024), lambda d, j: (d, 0, j)),
        ],
        out_specs=(
            pl.BlockSpec((1, TOK, 1024), lambda d, j: (d, 0, j)),
            pl.BlockSpec((1, 1, 2, TOK, HEAD), lambda d, j: (j, d, 0, 0, 0)),
            VMEM,
        ),
        scratch_shapes=[
            pltpu.VMEM((256, 1024), bf16),
            pltpu.VMEM((256, 1024), bf16),
            pltpu.VMEM((1024, HEAD), bf16),
            pltpu.VMEM((1024, HEAD), bf16),
            pltpu.VMEM((4, 4, 2, PRO, HEAD), f32),
        ],
        compiler_params=LOCAL,
        name="attention",
    )(info, everyone, keys, vals, Q, OG)


RETURN_COPIES = 8


def return_kernel(PP, QG, PS, QP, land, send, recv):
    me = Place()
    ring, partner = me.ring_zh(), me.partner()
    greet([ring[1], ring[2], partner])
    links = Links(send, recv)

    def add(dst, terms):
        for i in range(2):
            for d in range(2):
                total = terms[0][i, d].astype(f32)
                for term in terms[1:]:
                    total = total + term[i, d].astype(f32)
                dst[i, d] = total.astype(dst.dtype)

    going = Reduce4(
        links, ring, lambda c, h: PP.at[c, pl.ds(2 * h, 2)], lambda i: land.at[i], add
    )
    going.begin()
    queries = links.take()
    links.start(queries, QG.at[1 - me.core], QP, partner)
    going.mid()
    going.finish(lambda h: PS.at[pl.ds(2 * h, 2)])
    links.arrived(queries, QP, partner)
    links.drain()


def give_back(PP, QG):
    return pl.pallas_call(
        return_kernel,
        out_shape=(
            jax.ShapeDtypeStruct((4, 2, PRO, HEAD), f32),
            jax.ShapeDtypeStruct((TOK, 2048), bf16),
        ),
        in_specs=[VMEM, ANY],
        out_specs=(VMEM, ANY),
        scratch_shapes=[
            pltpu.VMEM((6, 2, 2, PRO, HEAD), bf16),
            pltpu.SemaphoreType.DMA((RETURN_COPIES,)),
            pltpu.SemaphoreType.DMA((RETURN_COPIES,)),
        ],
        compiler_params=remote_params(3),
        name="give_back",
    )(PP, QG)


W_STEP = 640


def weight_kernel(info, raw, RG, PS, cos, sin, gain, X, D, G, grads):
    step = pl.program_id(0)

    @pl.when(step == 0)
    def _():
        for d in range(2):
            c, s = tables_of(info, d, cos, sin)
            for j in range(2):
                cot = jnp.concatenate([RG[j, d, 0].astype(f32), PS[j, d]], 0)
                turned = (cot * c + swap_halves(cot * s)) * gain[...]
                k = raw[j, d]
                inverse = lax.rsqrt(jnp.mean(k * k, axis=1, keepdims=True) + 1e-06)
                along = jnp.mean(k * turned, axis=1, keepdims=True)
                back = inverse * turned - k * (inverse * inverse * inverse * along)
                grads[pl.ds(d * DEV, DEV), pl.ds(j * HEAD, HEAD)] = back.astype(bf16)
                values = jnp.concatenate([RG[j, d, 1], PS[2 + j, d].astype(bf16)], 0)
                grads[pl.ds(d * DEV, DEV), pl.ds((2 + j) * HEAD, HEAD)] = values
        G[0] = grads[:DEV]
        G[1] = grads[DEV:]

    rows = jnp.concatenate([X[0], X[1]], 0)
    term = lax.dot_general(
        rows, grads[...], (((0,), (0,)), ((), ())), preferred_element_type=f32
    ).astype(bf16)
    for t in range(4):
        D[t] = term[:, t * HEAD : (t + 1) * HEAD]


def weight_terms(info, raw, RG, PS, cos, sin, gain, X):
    return pl.pallas_call(
        weight_kernel,
        out_shape=(
            jax.ShapeDtypeStruct((4, WIDTH, HEAD), bf16),
            jax.ShapeDtypeStruct((2, DEV, 512), bf16),
        ),
        grid=(WIDTH // W_STEP,),
        in_specs=[SMEM] + [VMEM] * 6 + [pl.BlockSpec((2, DEV, W_STEP), lambda i: (0, 0, i))],
        out_specs=(pl.BlockSpec((4, W_STEP, HEAD), lambda i: (0, i, 0)), VMEM),
        scratch_shapes=[pltpu.VMEM((2 * DEV, 512), bf16)],
        compiler_params=LOCAL,
        name="weight_terms",
    )(info, raw, RG, PS, cos, sin, gain, X)


SUM_COPIES = 64


def sum_kernel(D, G, WG, GO, one, acc1, two, acc2, near, acc3, three, wg, send, recv):
    me = Place()
    partner = me.partner()
    near_minus, near_plus = me.near_z()
    ring_x, ring_y, ring_zh = me.ring_x(), me.ring_y(), me.ring_zh()
    greet([*ring_x[1:], *ring_y[1:], *ring_zh[1:], near_minus, near_plus, partner])
    links = Links(send, recv)
    core, zl = me.core, me.zl

    first, second = [], []
    for t in range(4):
        if t < 2:
            part = lambda c, h, t=t: D.at[t, :, c, h]
        else:
            part = lambda c, h, t=t: D.at[t, c, :, h]
        ring = ring_x if t < 2 else ring_y
        other = ring_y if t < 2 else ring_x
        first.append(Reduce4(links, ring, part, lambda i, t=t: one.at[t, i], add_blocks))
        second.append(
            Reduce4(
                links,
                other,
                lambda c, h, t=t: acc1.at[t, c, h],
                lambda i, t=t: two.at[t, i],
                add_block,
            )
        )
    order = (0, 2, 1, 3)
    for t in order:
        first[t].begin()
    grads = links.take()
    links.start(grads, G.at[1 - core], GO, partner)
    for t in order:
        first[t].mid()
    for t in order:
        first[t].finish(lambda h, t=t: acc1.at[t, :, h])
        second[t].begin()
    for t in order:
        second[t].mid()
    for t in order:
        second[t].finish(lambda h, t=t: acc2.at[t, h])

    up, down = links.take(), links.take()
    links.start(up, acc2.at[:, 1 - zl, pl.ds(0, HALF)], near.at[0], near_plus)
    links.start(down, acc2.at[:, 1 - zl, pl.ds(HALF, HALF)], near.at[1], near_minus)
    links.arrived(up, near.at[0], near_plus)
    add_blocks(acc3.at[:, 0], [acc2.at[:, zl, pl.ds(0, HALF)], near.at[0]])
    links.arrived(down, near.at[1], near_minus)
    add_blocks(acc3.at[:, 1], [acc2.at[:, zl, pl.ds(HALF, HALF)], near.at[1]])

    third = Reduce4(links, ring_zh, lambda c, h: acc3.at[c, h], lambda i: three.at[i], add_block)
    third.begin()
    third.mid()
    third.finish(lambda h: wg.at[core, me.zh, h])
    last = Gather4(links, ring_zh, lambda c: wg.at[core, c], lambda c, h: wg.at[core, c, h])
    last.begin()
    last.forward()
    last.finish()
    across = links.take()
    links.start(across, wg.at[core], wg.at[core], partner)
    links.arrived(across, wg.at[1 - core], partner)
    links.arrived(grads, GO, partner)
    WG[...] = wg[...]
    links.drain()
    assert links.used <= SUM_COPIES


def sum_terms(D, G):
    return pl.pallas_call(
        sum_kernel,
        out_shape=(
            jax.ShapeDtypeStruct((2, 4, 2, HALF, HEAD), bf16),
            jax.ShapeDtypeStruct((DEV, 512), bf16),
        ),
        in_specs=[VMEM, ANY],
        out_specs=(VMEM, ANY),
        scratch_shapes=[
            pltpu.VMEM((4, 6, 4, ROWS, HEAD), bf16),
            pltpu.VMEM((4, 4, 2, ROWS, HEAD), bf16),
            pltpu.VMEM((4, 6, ROWS, HEAD), bf16),
            pltpu.VMEM((4, 2, ROWS, HEAD), bf16),
            pltpu.VMEM((2, 4, HALF, HEAD), bf16),
            pltpu.VMEM((4, 2, HALF, HEAD), bf16),
            pltpu.VMEM((6, HALF, HEAD), bf16),
            pltpu.VMEM((2, 4, 2, HALF, HEAD), bf16),
            pltpu.SemaphoreType.DMA((SUM_COPIES,)),
            pltpu.SemaphoreType.DMA((SUM_COPIES,)),
        ],
        compiler_params=remote_params(4),
        name="sum_terms",
    )(D, G)


I_STEP = 640


def input_kernel(info, G, GO, W, W2, WG, QG, QP, resp, prompt, qgrad, kout, vout, sems):
    step = pl.program_id(0)
    core = info[0, 1, 0]
    mine = pl.ds(pl.multiple_of(core * 2048, 2048), 2048)
    theirs = pl.ds(pl.multiple_of((1 - core) * 2048, 2048), 2048)
    copies = (
        pltpu.make_async_copy(QG.at[core], qgrad.at[0, :, mine], sems.at[0]),
        pltpu.make_async_copy(QP, qgrad.at[0, :, theirs], sems.at[1]),
    )

    @pl.when(step == 0)
    def _():
        for made in copies:
            made.start()
        for c in range(2):
            for j in range(2):
                lanes = pl.ds((2 * c + j) * HEAD, HEAD)
                kout[:, lanes] = WG[c, j]
                vout[:, lanes] = WG[c, 2 + j]

    total = 0.0
    for grads, weights in ((G[core], W), (GO[...], W2)):
        both = jnp.concatenate([weights[t] for t in range(4)], 1)
        total = total + lax.dot_general(
            grads, both, (((1,), (1,)), ((), ())), preferred_element_type=f32
        )
    total = total.astype(bf16)
    resp[0] = total[:TOK]
    prompt[0] = total[TOK:]

    @pl.when(step == pl.num_programs(0) - 1)
    def _():
        for made in copies:
            made.wait()


def input_grads(info, G, GO, W, W2, WG, QG, QP):
    return pl.pallas_call(
        input_kernel,
        out_shape=(
            jax.ShapeDtypeStruct((1, TOK, WIDTH), bf16),
            jax.ShapeDtypeStruct((1, PRO, WIDTH), bf16),
            jax.ShapeDtypeStruct((1, TOK, 4096), bf16),
            jax.ShapeDtypeStruct((ROWS, 512), bf16),
            jax.ShapeDtypeStruct((ROWS, 512), bf16),
        ),
        grid=(WIDTH // I_STEP,),
        in_specs=[
            SMEM,
            VMEM,
            VMEM,
            pl.BlockSpec((4, I_STEP, HEAD), lambda i: (0, i, 0)),
            pl.BlockSpec((4, I_STEP, HEAD), lambda i: (0, i, 0)),
            VMEM,
            ANY,
            ANY,
        ],
        out_specs=(
            pl.BlockSpec((1, TOK, I_STEP), lambda i: (0, 0, i)),
            pl.BlockSpec((1, PRO, I_STEP), lambda i: (0, 0, i)),
            ANY,
            VMEM,
            VMEM,
        ),
        scratch_shapes=[pltpu.SemaphoreType.DMA((2,))],
        compiler_params=LOCAL,
        name="input_grads",
    )(info, G, GO, W, W2, WG, QG, QP)


def local(
    queries, out_grad, resp_in, prompt_in, key_matrix, value_matrix, key_gain, seg_prompt, seg_start, seg_len, owner
):
    cos, sin = rotary_tables()
    gain = key_gain.reshape(1, HEAD)
    match = seg_prompt[0][:, None] == jnp.arange(8, dtype=jnp.int32)[None, :]
    slots = jnp.sum(jnp.where(match, owner[0][None, :], 0), 1)
    line = jnp.concatenate([slots, seg_start[0], seg_len[0], jnp.zeros((122,), jnp.int32)])
    core = lax.rem(lax.axis_index("grp"), 2).astype(jnp.int32)
    info = jnp.concatenate([line[None], jnp.broadcast_to(core, (7, 128))], 0)

    W, X, Q, OG, both = gather(key_matrix, value_matrix, resp_in, prompt_in, queries, out_grad, info)
    flat = W.reshape(4, WIDTH, HEAD)
    raw, keys, vals, pkv = project(both, X, flat, cos, sin, gain)
    everyone, W2 = share(pkv, W)
    QG, RG, PP = attention(both, everyone, keys, vals, Q, OG)
    PS, QP = give_back(PP, QG)
    D, G = weight_terms(both, raw, RG, PS, cos, sin, gain, X)
    WG, GO = sum_terms(D.reshape(4, 4, 4, 2, ROWS, HEAD), G)
    WG = WG.reshape(2, 4, ROWS, HEAD)
    resp, prompt, qgrad, kout, vout = input_grads(
        info.reshape(1, 8, 128), G, GO, flat, W2.reshape(4, WIDTH, HEAD), WG, QG, QP
    )
    return qgrad, resp, prompt, kout, vout


def solution(mesh):
    in_specs = (
        P("fsdp", "grp", None),
        P("fsdp", "grp", None),
        P("fsdp", "grp", None),
        P("fsdp", "grp", None),
        P("fsdp", None),
        P("fsdp", None),
        P(),
        P("fsdp", "grp"),
        P("fsdp", "grp"),
        P("fsdp", "grp"),
        P("fsdp", None),
    )
    out_specs = (
        P("fsdp", "grp", None),
        P("fsdp", "grp", None),
        P("fsdp", "grp", None),
        P("fsdp", None),
        P("fsdp", None),
    )
    return jax.shard_map(local, mesh=mesh, in_specs=in_specs, out_specs=out_specs, check_vma=False)
```

time: 820 us -> 226 us (0.28)
  waiting for transfers between devices: 650 us -> 0 us
  Pallas kernels: 0 us -> 218 us
  blocking collectives: 53 us -> 0 us
  matrix products: 38.9 us -> 0 us
  local copies, waits for them, and re-layouts: 36.6 us -> 5.42 us
  other arithmetic: 23.9 us -> 1.61 us
  between operations: 16 us -> 0.73 us
    all_gather x2 -> x0, waiting for transfers between devices: 304 us -> none  [the longest x1 159 us: local(): whole_value = lax.all_gather(value_matrix, 'fsdp', axis=0, tiled=True)]
    reduce_scatter x1 -> x0, waiting for transfers between devices: 222 us -> none  [local(): lax.psum_scatter(lax.dot_general(all_rows, stacked, (((0,), (0,)), ((), (...]
    pallas_call x0 -> x8, Pallas kernels: none -> 218 us  [the longest x1 80.3 us: gather(): pl.pallas_call(gather_kernel, out_shape=(jax.ShapeDtypeStruct((4, 4, 4, 2...]
    psum x1 -> x0, waiting for transfers between devices: 70.1 us -> none  [local(): lax.psum(summed[:, :key_value_width].astype(jnp.bfloat16), 'grp')]
    unnamed x8 -> x0, waiting for transfers between devices: 53.3 us -> none
    all_gather x2 -> x0, blocking collectives: 53 us -> none  [the longest x1 38.1 us: local(): lax.all_gather(owned_keys, 'grp', axis=0, tiled=True)]
    dot_general x10 -> x0, matrix products: 38.9 us -> none  [the longest x2 8.98 us: back_project(): lax.dot_general(grads, weight, (((1,), (1,)), ((), ())), preferred_elemen...]
    unnamed x54 -> x16, local copies, waits for them, and re-layouts: 17.8 us -> 5.41 us
  transfers between devices with their start and end apart: 6 -> 0, of which waited for: 6 -> 0; matrix products, arithmetic and copies ran while one was open for 7% -> 0% of each run, Pallas kernels for 0% -> 0%
where the time goes in v1:
time: 226 us
  Pallas kernels  218 us (96%)
  local copies, waits for them, and re-layouts  5.42 us (2%)
    pallas_call x1, Pallas kernels, gather(): pl.pallas_call(gather_kernel, out_shape=(jax.ShapeDtypeStruct((4, 4, 4, 2...  80.3 us
    pallas_call x1, Pallas kernels, sum_terms(): pl.pallas_call(sum_kernel, out_shape=(jax.ShapeDtypeStruct((2, 4, 2, HALF...  62.3 us
    pallas_call x1, Pallas kernels, input_grads(): pl.pallas_call(input_kernel, out_shape=(jax.ShapeDtypeStruct((1, TOK, WID...  19.1 us
    pallas_call x1, Pallas kernels, share(): pl.pallas_call(share_kernel, out_shape=(jax.ShapeDtypeStruct((4, 4, 2, PR...  14.2 us
    pallas_call x1, Pallas kernels, attention(): pl.pallas_call(attention_kernel, out_shape=(jax.ShapeDtypeStruct((2, TOK,...  12.9 us
    pallas_call x1, Pallas kernels, give_back(): pl.pallas_call(return_kernel, out_shape=(jax.ShapeDtypeStruct((4, 2, PRO,...  12.7 us
    pallas_call x1, Pallas kernels, weight_terms(): pl.pallas_call(weight_kernel, out_shape=(jax.ShapeDtypeStruct((4, WIDTH,...  9.21 us
    pallas_call x1, Pallas kernels, project(): pl.pallas_call(project_kernel, out_shape=(jax.ShapeDtypeStruct((2, 2, DEV...  6.94 us

profile of v1, /device:TPU:1, one launch (start us, length us, event | category | flops | bytes accessed | tf_op | source)
XLA Modules:
  0.0 225.5 jit_solution(13105603603109664071)
XLA Ops:
  0.6 0.9 fusion
  1.5 0.8 add_bitcast_fusion
  2.3 0.0 copy-start
  2.3 1.1 copy-done
  3.3 0.0 copy-start.5
  3.3 0.9 copy-done.5
  4.3 0.0 copy-start.6
  4.3 0.9 copy-done.6
  5.2 80.3 %gather.1 = (bf16[4,4,4,2,160,128]{5,4,3,2,1,0:T(8,128)(2,1)}, bf16[2,192,5120]{2,1,0:T(8,128)(2,1)}, bf16[2,128,2048]{2,1,0:T(8,128)(2,1)}, bf16[2,128,2048]{2,1,0:T(8,128)(2,1)}, s32[2,8,128]{2,1,0:T(8,128)S(1)}) custom-call(bf16[160,512]{1,0:T(8,128)(2,1)S(1)} %copy-done.5, bf16[160,512]{1,0:T(8,128)(2,1)S(1)} %copy-done.6, bf16[1,128,5120]{2,1,0:T(8,128)(2,1)} %resp.1, ...), custom_call_target="tpu_custom_call" | custom-call | tf_op jit(solution)/shard_map/gather/pallas_call | solution.py:315
  85.5 0.0 copy-start.1
  85.5 0.9 copy-done.1
  86.4 0.0 copy-start.3
  86.5 0.9 copy-done.3
  87.4 0.0 copy-start.7
  87.4 0.7 copy-done.7
  88.0 6.9 %project.1 = (f32[2,2,192,128]{3,2,1,0:T(8,128)S(1)}, bf16[2,2,192,128]{3,2,1,0:T(8,128)(2,1)S(1)}, bf16[2,2,192,128]{3,2,1,0:T(8,128)(2,1)S(1)}, bf16[4,2,64,128]{3,2,1,0:T(8,128)(2,1)S(1)}) custom-call(s32[2,8,128]{2,1,0:T(8,128)S(1)} %get-tuple-element.30.info, bf16[2,192,5120]{2,1,0:T(8,128)(2,1)} %get-tuple-element.31.X, ...), custom_call_target="tpu_custom_call" | custom-call | tf_op jit(solution)/shard_map/project/pallas_call | solution.py:387
  95.0 0.0 copy-start.2
  95.0 0.0 copy-start.4
  95.0 14.2 %share.1 = (bf16[4,4,2,64,128]{4,3,2,1,0:T(8,128)(2,1)S(1)}, bf16[4,4,4,2,160,128]{5,4,3,2,1,0:T(8,128)(2,1)}) custom-call(bf16[4,2,64,128]{3,2,1,0:T(8,128)(2,1)S(1)} %get-tuple-element.34.pkv, bf16[4,4,4,2,160,128]{5,4,3,2,1,0:T(8,128)(2,1)} %get-tuple-element.32.W), custom_call_target="tpu_custom_call" | custom-call | tf_op jit(solution)/shard_map/share/pallas_call | solution.py:435
  109.2 12.9 %attention.1 = (bf16[2,128,2048]{2,1,0:T(8,128)(2,1)}, bf16[2,2,2,128,128]{4,3,2,1,0:T(8,128)(2,1)S(1)}, bf16[4,4,2,64,128]{4,3,2,1,0:T(8,128)(2,1)S(1)}) custom-call(s32[2,8,128]{2,1,0:T(8,128)S(1)} %get-tuple-element.30.info, bf16[4,4,2,64,128]{4,3,2,1,0:T(8,128)(2,1)S(1)} %get-tuple-element.35.everyone, ...), custom_call_target="tpu_custom_call" | custom-call | tf_op jit(solution)/shard_map/attention/pallas_call | solution.py:512
  122.1 12.7 %give_back.1 = (f32[4,2,64,128]{3,2,1,0:T(8,128)S(1)}, bf16[128,2048]{1,0:T(8,128)(2,1)S(1)}) custom-call(bf16[4,4,2,64,128]{4,3,2,1,0:T(8,128)(2,1)S(1)} %get-tuple-element.41.PP, bf16[2,128,2048]{2,1,0:T(8,128)(2,1)} %get-tuple-element.42.QG), custom_call_target="tpu_custom_call" | custom-call | tf_op jit(solution)/shard_map/give_back/pallas_call | solution.py:575
  134.8 0.0 copy-done.2
  134.8 0.0 copy-done.4
  134.8 9.2 %weight_terms.1 = (bf16[4,5120,128]{2,1,0:T(8,128)(2,1)}, bf16[2,192,512]{2,1,0:T(8,128)(2,1)S(1)}) custom-call(s32[2,8,128]{2,1,0:T(8,128)S(1)} %get-tuple-element.30.info, f32[2,2,192,128]{3,2,1,0:T(8,128)S(1)} %get-tuple-element.33.raw, bf16[2,2,2,128,128]{4,3,2,1,0:T(8,128)(2,1)S(1)} %get-tuple-element.40.RG, ...), custom_call_target="tpu_custom_call" | custom-call | tf_op jit(solution)/shard_map/weight_terms/pallas_call | solution.py:625
  144.1 62.3 %sum_terms.1 = (bf16[2,4,2,80,128]{4,3,2,1,0:T(8,128)(2,1)S(1)}, bf16[192,512]{1,0:T(8,128)(2,1)S(1)}) custom-call(bf16[4,4,4,2,160,128]{5,4,3,2,1,0:T(8,128)(2,1)} %bitcast.19, bf16[2,192,512]{2,1,0:T(8,128)(2,1)S(1)} %get-tuple-element.44.G), custom_call_target="tpu_custom_call" | custom-call | tf_op jit(solution)/shard_map/sum_terms/pallas_call | solution.py:711
  206.4 19.1 %input_grads.1 = (bf16[1,128,5120]{2,1,0:T(8,128)(2,1)}, bf16[1,64,5120]{2,1,0:T(8,128)(2,1)}, bf16[1,128,4096]{2,1,0:T(8,128)(2,1)}, bf16[160,512]{1,0:T(8,128)(2,1)}, bf16[160,512]{1,0:T(8,128)(2,1)}) custom-call(s32[1,8,128]{2,1,0:T(8,128)S(1)} %get-tuple-element.56.info, bf16[2,192,512]{2,1,0:T(8,128)(2,1)S(1)} %get-tuple-element.44.G, ...), custom_call_target="tpu_custom_call" | custom-call | tf_op jit(solution)/shard_map/input_grads/pallas_call | solution.py:776
  (2 shorter events, 0.0 us)
Async XLA Ops:
  2.3 1.1 copy-start
  3.3 0.9 copy-start.5
  4.3 0.9 copy-start.6
  85.5 0.9 copy-start.1
  86.4 0.9 copy-start.3
  87.4 0.7 copy-start.7
  95.0 39.9 %copy-start.2 = (f32[320,128]{1,0:T(8,128)S(1)}, f32[320,128]{1,0:T(8,128)}, u32[]{:S(2)}) copy-start(f32[320,128]{1,0:T(8,128)} %constant.18.clone.sin) | copy-start | bytes 491524
  95.0 39.9 %copy-start.4 = (f32[320,128]{1,0:T(8,128)S(1)}, f32[320,128]{1,0:T(8,128)}, u32[]{:S(2)}) copy-start(f32[320,128]{1,0:T(8,128)} %constant.17.clone.cos) | copy-start | bytes 491524
